TPU v7x, 32 devices: a whole 2x2x4 slice. The times are simulated.
32 devices in a mesh: groups: 2 (over y), dp: 4 (over z), tensor: 4 (over x, core).
Axes of the slice: x: 2, y: 2, z: 4, core: 2. Of those that a mesh axis runs over, the one named last changes fastest.
Arguments:
- train_acts: bfloat16 [2048, 28672], P(('groups', 'dp'), 'tensor'), parts along dimension 0, may hold values from -6 to 6
- train_grads: bfloat16 [2048, 8192], P(('groups', 'dp'), 'tensor'), parts along dimension 0, may hold values from -6 to 6
- train_lengths: int32 [16], P(('groups', 'dp')), parts along dimension 0, may hold values from 32 to 128, as said below
- proj_in: bfloat16 [28672, 64], P('tensor'), may hold values from -0.03125 to 0.03125
- proj_out: bfloat16 [8192, 64], P('tensor'), may hold values from -0.0625 to 0.0625
- query_sketch: float32 [512, 4096], P(('groups', 'dp')), parts along dimension 0, may hold values from -6 to 6
- precond_in: float32 [64, 64], replicated
- precond_out: float32 [64, 64], replicated
Outputs:
- scores: float32 [16, 256], P(('groups', 'dp')), parts along dimension 0
There are 2 independent parts, one for each index of `groups`. A program takes and returns all parts, laid end to end along the dimension named above; an argument that names none is the same for every part. Nothing has to cross between parts.
Inputs may be any that keep to these rules, and one draw needn't show every extreme that they name: `train_lengths`: each training sequence has at least 32 valid tokens; some sequence has all 128.
All inputs are finite; a program needn't handle non-finite values.
Results may differ from a plain program's by a relative error of at most 0.0003.
Values sent between devices are 32-bit elements; how exact they have to be, the bound alone decides.
A program may use at most 64 MiB of HBM per device.

v0:
```python
import math

import jax
import jax.numpy as jnp
from jax import lax
from jax.sharding import PartitionSpec as P


def local(
    train_acts, train_grads, train_lengths, proj_in, proj_out, query_sketch, precond_in, precond_out
):
    tokens = train_acts.shape[0]
    count = train_lengths.shape[0]
    seq_len = tokens // count
    width_in = proj_in.shape[1]
    width_out = proj_out.shape[1]
    part_left = jnp.dot(train_acts, proj_in, preferred_element_type=jnp.float32)
    part_right = jnp.dot(train_grads, proj_out, preferred_element_type=jnp.float32)
    partial_value = jnp.concatenate([part_left, part_right], axis=1)
    summed = lax.psum(partial_value, "tensor")
    slots = jnp.arange(seq_len, dtype=jnp.int32)
    keep = (slots[None, :] < train_lengths[:, None]).astype(jnp.float32)
    left_seq = summed[:, :width_in].reshape(count, seq_len, width_in) * keep[:, :, None]
    right_seq = summed[:, width_in:].reshape(count, seq_len, width_out)
    sketch = jnp.einsum("sti,stj->sij", left_seq, right_seq, precision=lax.Precision.HIGHEST)
    sketch = sketch * jnp.float32(1.0 / math.sqrt(seq_len))
    flat_sketch = sketch.reshape(count, width_in * width_out)
    queries_here = query_sketch.shape[0]
    raw = query_sketch.reshape(queries_here, width_in, width_out)
    leftmul = jnp.einsum("ik,nkl->nil", precond_in, raw, precision=lax.Precision.HIGHEST)
    cond = jnp.einsum("nil,lj->nij", leftmul, precond_out, precision=lax.Precision.HIGHEST)
    cond = cond.reshape(queries_here, width_in * width_out)
    column_block = lax.dot_general(
        lax.all_gather(flat_sketch, "dp", axis=0, tiled=True),
        cond,
        (((1,), (1,)), ((), ())),
        precision=lax.Precision.HIGHEST,
    )
    scores = lax.all_to_all(column_block, "dp", split_axis=0, concat_axis=1, tiled=True)
    return scores * jnp.float32(1.0 / math.sqrt(width_in * width_out))


def solution(mesh):
    placed = (
        P(("groups", "dp"), "tensor"),
        P(("groups", "dp"), "tensor"),
        P(("groups", "dp")),
        P("tensor", None),
        P("tensor", None),
        P(("groups", "dp"), None),
        P(),
        P(),
    )
    return jax.shard_map(
        local, mesh=mesh, in_specs=placed, out_specs=P(("groups", "dp"), None), check_vma=False
    )
```

profile of v0, /device:TPU:0, one launch (start us, length us, event | category | flops | bytes accessed | tf_op | source)
XLA Modules:
  0.0 83.4 jit_solution(4884212366184307998)
XLA Ops:
  6.5 0.0 copy-start
  6.5 0.0 all-reduce.2.cloned.1.call-start
  6.5 1.2 %copy-done = bf16[256,2048]{1,0:T(8,128)(2,1)S(1)} copy-done((bf16[256,2048]{1,0:T(8,128)(2,1)S(1)}, bf16[256,2048]{1,0:T(8,128)(2,1)}, u32[]{:S(2)}) %copy-start) | copy-done | bytes 1048600
  7.8 1.4 %fusion.10 = f32[256,64]{0,1:T(8,128)S(1)} fusion(bf16[256,2048]{1,0:T(8,128)(2,1)S(1)} %copy-done, bf16[2048,64]{0,1:T(8,128)(2,1)} %param.12), kind=kOutput, calls=%fused_computation.17 | convolution fusion | flops 67108864 | bytes 1376256 | tf_op jit(solution)/shard_map/dot_general | solution.py:18
  9.2 3.5 %fusion.9 = f32[256,64]{0,1:T(8,128)S(1)} fusion(bf16[256,7168]{1,0:T(8,128)(2,1)} %param.8, bf16[7168,64]{0,1:T(8,128)(2,1)} %param.11), kind=kOutput, calls=%fused_computation.16 | convolution fusion | flops 234881024 | bytes 4653056 | tf_op jit(solution)/shard_map/dot_general | solution.py:17
  12.7 0.0 copy-start.1
  12.7 0.7 pad_maximum_fusion
  13.3 0.0 all-reduce.2.cloned.1.call-update
  13.4 2.0 %reshape.46 = f32[64,64,64]{2,1,0:T(8,128)S(1)} reshape(f32[64,4096]{1,0:T(8,128)} %param.13) | data formatting | bytes 2097152 | tf_op jit(solution)/shard_map/reshape | solution.py:29
  15.4 0.0 copy-done.1
  15.4 0.0 copy-start.2
  15.4 3.5 %fusion.6 = f32[64,64,64]{2,1,0:T(8,128)S(1)} fusion(f32[64,64,64]{2,1,0:T(8,128)S(1)} %reshape.46, f32[64,64]{1,0:T(8,128)S(1)} %copy-done.1), kind=kOutput, calls=%fused_computation.11 | convolution fusion | flops 201326592 | bytes 2113536 | tf_op jit(solution)/shard_map/ik,nkl->nil/dot_general | solution.py:30
  18.9 0.0 copy-done.2
  18.9 0.0 copy-start.3
  19.0 3.5 %fusion = f32[64,64,64]{2,1,0:T(8,128)S(1)} fusion(f32[64,64,64]{2,1,0:T(8,128)S(1)} %fusion.6, f32[64,64]{1,0:T(8,128)S(1)} %copy-done.2), kind=kOutput, calls=%fused_computation | convolution fusion | flops 201326592 | bytes 2113536 | tf_op jit(solution)/shard_map/nil,lj->nij/dot_general | solution.py:31
  22.5 0.0 copy-done.3
  22.5 0.1 compare_convert_fusion
  22.5 1.6 %reshape.54 = f32[64,4096,1]{1,0,2:T(8,128)} reshape(f32[64,64,64]{2,1,0:T(8,128)S(1)} %fusion) | data formatting | bytes 2097152 | tf_op jit(solution)/shard_map/reshape | solution.py:32
  24.2 23.5 %all-reduce.2.cloned.1.call-done = f32[256,128]{0,1:T(8,128)} async-done(((f32[256,128]{0,1:T(8,128)}), f32[256,128]{0,1:T(8,128)}) %all-reduce.2.cloned.1.call-update) | async-done | bytes 131088 | tf_op jit(solution)/shard_map/psum | solution.py:20
  47.6 0.9 %slice_bitcast_fusion.1 = (f32[8,2,8,128]{3,2,1,0:T(8,128)S(1)}, f32[8,2,8,128]{3,2,1,0:T(8,128)S(1)}) fusion(f32[256,128]{0,1:T(8,128)} %all-reduce.2.cloned.1.call-done), kind=kLoop, calls=%fused_computation.9 | loop fusion | bytes 262144
  48.5 0.2 convolution_multiply_fusion
  48.7 0.1 reshape.48
  48.8 13.4 %all-gather = f32[4,2,4096]{2,1,0:T(2,128)S(1)} all-gather(f32[1,2,4096]{2,1,0:T(2,128)S(1)} %reshape.48), channel_id=1, replica_groups=mesh['groups'=2,'dp'=4,'tensor'=4] {'dp'}, dimensions={0}, use_global_device_ids=true | all-gather | bytes 163840 | tf_op jit(solution)/shard_map/all_gather | solution.py:34
  62.3 2.3 %fusion.11 = f32[4,2,64]{2,1,0:T(2,128)S(1)} fusion(f32[4,2,4096]{2,1,0:T(2,128)S(1)} %all-gather, f32[64,4096,1]{1,0,2:T(8,128)} %reshape.54), kind=kOutput, calls=%fused_computation.18 | convolution fusion | flops 25165824 | bytes 1181696 | tf_op jit(solution)/shard_map/dot_general | solution.py:33
  64.6 0.1 reshape.56
  64.7 9.9 %all_to_all.10 = f32[4,1,128]{2,1,0:T(1,128)S(1)} all-to-all(f32[4,1,128]{2,1,0:T(1,128)S(1)} %reshape.56), channel_id=1, replica_groups=mesh['groups'=2,'dp'=4,'tensor'=4] {'dp'}, dimensions={0} | all-to-all | bytes 4096 | tf_op jit(solution)/shard_map/all_to_all | solution.py:39
  74.6 0.5 broadcast.18
  75.1 0.7 reduce
  75.8 0.1 reshape.57
  75.9 0.7 mul.33
  (2 shorter events, 0.0 us)
Async XLA Ops:
  6.5 1.2 %copy-start = (bf16[256,2048]{1,0:T(8,128)(2,1)S(1)}, bf16[256,2048]{1,0:T(8,128)(2,1)}, u32[]{:S(2)}) copy-start(bf16[256,2048]{1,0:T(8,128)(2,1)} %param.9) | copy-start | bytes 3145732
  6.5 41.1 %all-reduce.2.cloned.1.call-start = ((), (), s32[]{:S(2)}) async-start(), calls=%async_computation.1 | async-start | bytes 262144 | tf_op jit(solution)/shard_map/psum | solution.py:20
  12.7 2.7 %copy-start.1 = (f32[64,64]{1,0:T(8,128)S(1)}, f32[64,64]{1,0:T(8,128)}, u32[]{:S(2)}) copy-start(f32[64,64]{1,0:T(8,128)} %param.14) | copy-start | bytes 49156
  15.4 3.5 %copy-start.2 = (f32[64,64]{1,0:T(8,128)S(1)}, f32[64,64]{1,0:T(8,128)}, u32[]{:S(2)}) copy-start(f32[64,64]{1,0:T(8,128)} %param.15) | copy-start | bytes 49156
  18.9 3.5 %copy-start.3 = (s32[2]{0:T(128)S(1)}, s32[2]{0:T(128)}, u32[]{:S(2)}) copy-start(s32[2]{0:T(128)} %param.10) | copy-start | bytes 28
Sparse Core Ops, SparseCore 0:
  13.5 34.0 all-reduce.1
where the time goes:
time: 83.7 us; the launch traced here: 83.4 us
  waiting for transfers between devices  23.5 us (28%)
  blocking collectives  23.3 us (28%)
  matrix products  14.5 us (17%)
  between operations  13.5 us (16%)
  local copies, waits for them, and re-layouts  7.19 us (9%)
  other arithmetic  1.41 us (2%)
    psum x1, waiting for transfers between devices, local(): summed = lax.psum(partial_value, 'tensor')  23.5 us
    all_gather x1, blocking collectives, local(): lax.all_gather(flat_sketch, 'dp', axis=0, tiled=True)  13.4 us
    all_to_all x1, blocking collectives, local(): lax.all_to_all(column_block, 'dp', split_axis=0, concat_axis=1, tiled=True)  9.91 us
    dot_general x1, matrix products, local(): jnp.einsum('ik,nkl->nil', precond_in, raw, precision=lax.Precision.HIGHEST)  3.52 us
    dot_general x1, matrix products, local(): part_left = jnp.dot(train_acts, proj_in, preferred_element_type=jnp.float32)  3.52 us
    dot_general x1, matrix products, local(): jnp.einsum('nil,lj->nij', leftmul, precond_out, precision=lax.Precision.H...  3.49 us
    unnamed x12, local copies, waits for them, and re-layouts  2.38 us
    dot_general x1, matrix products, local(): lax.dot_general(lax.all_gather(flat_sketch, 'dp', axis=0, tiled=True), co...  2.33 us
  transfers between devices with their start and end apart: 1, of which 1 were waited for; matrix products, arithmetic and copies ran while one was open for 13% of the time, Pallas kernels for 0%

commit v1 on v0

v1 whole, which is shorter than its diff:
```python
import functools
import math

import jax
import jax.numpy as jnp
from jax import lax
from jax.experimental import pallas as pl
from jax.experimental.pallas import tpu as pltpu
from jax.sharding import PartitionSpec as P

HIGH = lax.Precision.HIGHEST
MESH = pl.DeviceIdType.MESH
NT = (((1,), (1,)), ((), ()))
NN = (((1,), (0,)), ((), ()))


def f32dot(a, b, dims):
    return lax.dot_general(a, b, dims, precision=HIGH, preferred_element_type=jnp.float32)


def bf16dot(a, b):
    return lax.dot_general(a, b, NT, preferred_element_type=jnp.float32)


def loop(low, high, body):
    if high - low <= 4:
        for i in range(low, high):
            body(i)
    else:
        def step(i, carry):
            body(i)
            return carry
        lax.fori_loop(low, high, step, 0)


def kernel(
    nd, nt, seq_len, scale,
    lengths, acts, grads, pin, pout, query, pre_in, pre_out,
    out,
    acts_v, grads_v, pin_v, pout_v, query_v, pre_in_v, pre_out_v,
    part, got, gather, rows, final,
    load_sem, send_a, recv_a, send_b, recv_b, send_c, recv_c,
):
    d = lax.axis_index("dp")
    t = lax.axis_index("tensor")
    width = pin.shape[0]
    half = width // 2
    tok = acts.shape[0] // nt
    count = out.shape[0]
    nq = query.shape[0]
    total = nd * nt

    def place(k):
        chips = nt // 2
        return ((t // 2 + chips - 1 - k // 2) % chips) * 2 + (t % 2 + 1 - k % 2) % 2

    fixed = [
        pltpu.make_async_copy(src, dst, load_sem.at[2 * nt + i])
        for i, (src, dst) in enumerate(
            [(pre_in, pre_in_v), (pre_out, pre_out_v), (pin, pin_v), (pout, pout_v), (query, query_v)]
        )
    ]
    for copy in fixed[:4]:
        copy.start()
    loads = []
    for k in range(nt):
        chunk = pl.ds(pl.multiple_of(place(k) * tok, tok), tok)
        loads.append((
            pltpu.make_async_copy(acts.at[chunk, :], acts_v.at[k], load_sem.at[2 * k]),
            pltpu.make_async_copy(grads.at[chunk, :], grads_v.at[k], load_sem.at[2 * k + 1]),
        ))
        for copy in loads[k]:
            copy.start()
    fixed[4].start()

    barrier = pltpu.get_barrier_semaphore()

    def greet(i):
        other = (d * nt + t + i) % total
        pl.semaphore_signal(
            barrier, inc=1, device_id={"dp": other // nt, "tensor": other % nt}, device_id_type=MESH
        )

    if total <= 16:
        for i in range(1, total):
            greet(i)
    else:
        loop(1, total, greet)

    for copy in fixed[:2]:
        copy.wait()
    r = lax.broadcasted_iota(jnp.int32, (width, width), 0)
    c = lax.broadcasted_iota(jnp.int32, (width, width), 1)
    pick = jnp.where(c == jnp.where(r < half, 2 * r, 2 * (r - half) + 1), 1.0, 0.0).astype(jnp.float32)
    pre_t = f32dot(pick, pre_in_v[...], NT)

    for copy in fixed[2:4]:
        copy.wait()
    sends = []
    for k in range(nt):
        for copy in loads[k]:
            copy.wait()
        part[k, 0:width, 0:tok] = bf16dot(pin_v[...], acts_v[k])
        part[k, 0:tok, tok : tok + width] = bf16dot(grads_v[k], pout_v[...])
        if k == 0:
            pl.semaphore_wait(barrier, total - 1)
        if k < nt - 1:
            copy = pltpu.make_async_remote_copy(
                src_ref=part.at[k], dst_ref=got.at[k], send_sem=send_a.at[k], recv_sem=recv_a.at[k],
                device_id={"tensor": place(k)}, device_id_type=MESH,
            )
            copy.start()
            sends.append(copy)
    fixed[4].wait()

    left = part[nt - 1, 0:width, 0:tok]
    right = part[nt - 1, 0:tok, tok : tok + width]
    for k in range(nt - 2, -1, -1):
        sends[k].wait_recv()
        left = left + got[k, 0:width, 0:tok]
        right = right + got[k, 0:tok, tok : tok + width]
    start = t * tok
    length = lengths[start // seq_len]
    slot = lax.broadcasted_iota(jnp.int32, (width, tok), 1) + start % seq_len
    left = jnp.where(slot < length, left, 0.0)
    u = f32dot(pre_t, left, NN)
    w = f32dot(right, pre_out_v[...], NT)
    g = f32dot(u, w, NN)
    gather[0] = jnp.concatenate([g[:half], g[half:]], axis=1)

    def gather_copy(j):
        return pltpu.make_async_remote_copy(
            src_ref=gather.at[0], dst_ref=gather.at[j], send_sem=send_b.at[j], recv_sem=recv_b.at[j],
            device_id={"dp": (d + j) % nd}, device_id_type=MESH,
        )

    loop(1, nd, lambda j: gather_copy(j).start())

    ones = jnp.ones((8, 2 * width), jnp.float32)
    mine = d * nt + t

    def score(j):
        acc = jnp.zeros((nq, 2 * width), jnp.float32)
        for p in range(half):
            acc = acc + query_v[:, 2 * width * p : 2 * width * (p + 1)] * gather[j, p : p + 1, :]
        row = f32dot(ones, acc, NT)[0:1] * scale
        rows[j] = jnp.concatenate([row, row], axis=1)

    def row_copy(j, to):
        return pltpu.make_async_remote_copy(
            src_ref=rows.at[j], dst_ref=final.at[mine], send_sem=send_c, recv_sem=recv_c,
            device_id={"dp": (d + nd - j) % nd, "tensor": to}, device_id_type=MESH,
        )

    score(0)
    final[mine] = rows[0]
    loop(1, nt, lambda k: row_copy(0, (t + k) % nt).start())

    def step(j):
        gather_copy(j).wait_recv()
        score(j)
        loop(0, nt, lambda k: row_copy(j, (t + k) % nt).start())

    loop(1, nd, step)

    for copy in sends:
        copy.wait_send()
    loop(1, nd, lambda j: gather_copy(j).wait_send())
    most = final.at[pl.ds(0, total - 1)]
    pltpu.make_async_copy(most, most, send_c).wait()
    pltpu.make_async_copy(most, most, recv_c).wait()

    share = nt // count
    lane = lax.broadcasted_iota(jnp.int32, (1, 2 * nq), 1)
    for s in range(count):
        for pair in range(nd // 2):
            sums = []
            for e in range(2):
                base = (2 * pair + e) * nt + s * share
                value = final[base]
                for i in range(1, share):
                    value = value + final[base + i]
                sums.append(value)
            out[s : s + 1, 2 * nq * pair : 2 * nq * (pair + 1)] = jnp.where(lane < nq, sums[0], sums[1])


def solution(mesh):
    nd, nt = mesh.shape["dp"], mesh.shape["tensor"]

    def local(acts, grads, lengths, pin, pout, query, pre_in, pre_out):
        tokens, deep_in = acts.shape
        deep_out = grads.shape[1]
        count = lengths.shape[0]
        width = pin.shape[1]
        nq = query.shape[0]
        tok = tokens // nt
        seq_len = tokens // count
        scale = 1.0 / math.sqrt(seq_len) / math.sqrt(width * width)
        box = (max(width, tok), tok + width)
        anywhere = pl.BlockSpec(memory_space=pltpu.HBM)
        f32 = jnp.float32
        dma = pltpu.SemaphoreType.DMA
        return pl.pallas_call(
            functools.partial(kernel, nd, nt, seq_len, scale),
            out_shape=jax.ShapeDtypeStruct((count, nd * nq), f32),
            in_specs=[pl.BlockSpec(memory_space=pltpu.SMEM)] + [anywhere] * 7,
            out_specs=pl.BlockSpec(memory_space=pltpu.VMEM),
            scratch_shapes=[
                pltpu.VMEM((nt, tok, deep_in), acts.dtype),
                pltpu.VMEM((nt, tok, deep_out), grads.dtype),
                pltpu.VMEM((width, deep_in), pin.dtype),
                pltpu.VMEM((width, deep_out), pout.dtype),
                pltpu.VMEM(query.shape, f32),
                pltpu.VMEM(pre_in.shape, f32),
                pltpu.VMEM(pre_out.shape, f32),
                pltpu.VMEM((nt,) + box, f32),
                pltpu.VMEM((nt - 1,) + box, f32),
                pltpu.VMEM((nd, width // 2, 2 * width), f32),
                pltpu.VMEM((nd, 1, 2 * nq), f32),
                pltpu.VMEM((nd * nt, 1, 2 * nq), f32),
                dma((2 * nt + 5,)), dma((nt - 1,)), dma((nt - 1,)), dma((nd,)), dma((nd,)), dma, dma,
            ],
            compiler_params=pltpu.CompilerParams(
                collective_id=0, has_side_effects=True, vmem_limit_bytes=48 * 1024 * 1024
            ),
        )(lengths, acts, grads, pin.T, pout.T, query, pre_in, pre_out)

    placed = (
        P(("groups", "dp"), "tensor"),
        P(("groups", "dp"), "tensor"),
        P(("groups", "dp")),
        P("tensor", None),
        P("tensor", None),
        P(("groups", "dp"), None),
        P(),
        P(),
    )
    return jax.shard_map(
        local, mesh=mesh, in_specs=placed, out_specs=P(("groups", "dp"), None), check_vma=False
    )
```

time: 83.7 us -> 27.4 us (0.33)
  waiting for transfers between devices: 23.5 us -> 0 us
  blocking collectives: 23.3 us -> 0 us
  Pallas kernels: 0 us -> 19.7 us
  matrix products: 14.5 us -> 0 us
  between operations: 13.5 us -> 0.02 us
  other arithmetic: 1.41 us -> 0 us
    psum x1 -> x0, waiting for transfers between devices: 23.5 us -> none  [local(): summed = lax.psum(partial_value, 'tensor')]
    pallas_call x0 -> x1, Pallas kernels: none -> 19.7 us  [local(): pl.pallas_call(functools.partial(kernel, nd, nt, seq_len, scale), out_sha...]
    dot_general x6 -> x0, matrix products: 14.5 us -> none  [the longest x1 3.52 us: local(): jnp.einsum('ik,nkl->nil', precond_in, raw, precision=lax.Precision.HIGHEST)]
    all_gather x1 -> x0, blocking collectives: 13.4 us -> none  [local(): lax.all_gather(flat_sketch, 'dp', axis=0, tiled=True)]
    all_to_all x1 -> x0, blocking collectives: 9.91 us -> none  [local(): lax.all_to_all(column_block, 'dp', split_axis=0, concat_axis=1, tiled=True)]
    unnamed x12 -> x15, local copies, waits for them, and re-layouts: 2.38 us -> 7.33 us
    reshape x2 -> x0, local copies, waits for them, and re-layouts: 3.63 us -> none  [the longest x1 2 us: local(): raw = query_sketch.reshape(queries_here, width_in, width_out)]
  transfers between devices with their start and end apart: 1 -> 0, of which waited for: 1 -> 0; matrix products, arithmetic and copies ran while one was open for 13% -> 0% of each run, Pallas kernels for 0% -> 0%
where the time goes in v1:
time: 27.4 us; the launch traced here: 27 us
  Pallas kernels  19.7 us (72%)
  local copies, waits for them, and re-layouts  7.33 us (27%)
    pallas_call x1, Pallas kernels, local(): pl.pallas_call(functools.partial(kernel, nd, nt, seq_len, scale), out_sha...  19.7 us
    unnamed x15, local copies, waits for them, and re-layouts  7.33 us

profile of v1, /device:TPU:0, one launch (start us, length us, event | category | flops | bytes accessed | tf_op | source)
XLA Modules:
  0.0 27.0 jit_solution(247533009713225544)
XLA Ops:
  0.0 0.0 copy-start
  0.0 1.2 %copy-done = bf16[256,2048]{1,0:T(8,128)(2,1)S(1)} copy-done((bf16[256,2048]{1,0:T(8,128)(2,1)S(1)}, bf16[256,2048]{1,0:T(8,128)(2,1)}, u32[]{:S(2)}) %copy-start) | copy-done | bytes 1048600
  1.2 0.0 copy-start.1
  1.2 1.2 %copy-done.1 = f32[64,4096]{1,0:T(8,128)S(1)} copy-done((f32[64,4096]{1,0:T(8,128)S(1)}, f32[64,4096]{1,0:T(8,128)}, u32[]{:S(2)}) %copy-start.1) | copy-done | bytes 1048600
  2.5 0.0 copy-start.2
  2.5 1.2 %copy-done.2 = bf16[7168,64]{0,1:T(8,128)(2,1)S(1)} copy-done((bf16[7168,64]{0,1:T(8,128)(2,1)S(1)}, bf16[7168,64]{0,1:T(8,128)(2,1)}, u32[]{:S(2)}) %copy-start.2) | copy-done | bytes 917528
  3.6 0.0 copy-start.3
  3.6 0.9 %copy-done.3 = bf16[2048,64]{0,1:T(8,128)(2,1)S(1)} copy-done((bf16[2048,64]{0,1:T(8,128)(2,1)S(1)}, bf16[2048,64]{0,1:T(8,128)(2,1)}, u32[]{:S(2)}) %copy-start.3) | copy-done | bytes 262168
  4.6 0.0 copy-start.4
  4.6 0.8 %copy-done.4 = f32[64,64]{1,0:T(8,128)S(1)} copy-done((f32[64,64]{1,0:T(8,128)S(1)}, f32[64,64]{1,0:T(8,128)}, u32[]{:S(2)}) %copy-start.4) | copy-done | bytes 16408
  5.3 0.0 copy-start.5
  5.3 0.8 %copy-done.5 = f32[64,64]{1,0:T(8,128)S(1)} copy-done((f32[64,64]{1,0:T(8,128)S(1)}, f32[64,64]{1,0:T(8,128)}, u32[]{:S(2)}) %copy-start.5) | copy-done | bytes 16408
  6.1 0.0 copy-start.6
  6.1 0.7 %copy-done.6 = s32[2]{0:T(128)S(1)} copy-done((s32[2]{0:T(128)S(1)}, s32[2]{0:T(128)}, u32[]{:S(2)}) %copy-start.6) | copy-done | bytes 32
  6.8 19.7 %shard_map.82 = f32[2,256]{1,0:T(2,128)S(1)} custom-call(s32[2]{0:T(128)S(1)} %copy-done.6, bf16[256,7168]{1,0:T(8,128)(2,1)} %acts.1, bf16[256,2048]{1,0:T(8,128)(2,1)S(1)} %copy-done, bf16[64,7168]{1,0:T(8,128)(2,1)S(1)} %bitcast.2, bf16[64,2048]{1,0:T(8,128)(2,1)S(1)} %bitcast.3, f32[64,4096]{1,0:T(8,128)S(1)} %copy-done.1, f32[64,64]{1,0:T(8,128)S(1)} %copy-done.4, ...), custom_call_target="tpu_custom_call" | custom-call | tf_op jit(solution)/shard_map/pallas_call | solution.py:203
  26.4 0.6 %copy.10 = f32[2,256]{1,0:T(2,128)} copy(f32[2,256]{1,0:T(2,128)S(1)} %shard_map.82) | data formatting | bytes 4096
Async XLA Ops:
  0.0 1.2 %copy-start = (bf16[256,2048]{1,0:T(8,128)(2,1)S(1)}, bf16[256,2048]{1,0:T(8,128)(2,1)}, u32[]{:S(2)}) copy-start(bf16[256,2048]{1,0:T(8,128)(2,1)} %grads.1) | copy-start | bytes 3145732
  1.2 1.2 %copy-start.1 = (f32[64,4096]{1,0:T(8,128)S(1)}, f32[64,4096]{1,0:T(8,128)}, u32[]{:S(2)}) copy-start(f32[64,4096]{1,0:T(8,128)} %query.1) | copy-start | bytes 3145732
  2.5 1.2 %copy-start.2 = (bf16[7168,64]{0,1:T(8,128)(2,1)S(1)}, bf16[7168,64]{0,1:T(8,128)(2,1)}, u32[]{:S(2)}) copy-start(bf16[7168,64]{0,1:T(8,128)(2,1)} %param.11) | copy-start | bytes 2752516
  3.6 0.9 %copy-start.3 = (bf16[2048,64]{0,1:T(8,128)(2,1)S(1)}, bf16[2048,64]{0,1:T(8,128)(2,1)}, u32[]{:S(2)}) copy-start(bf16[2048,64]{0,1:T(8,128)(2,1)} %param.12) | copy-start | bytes 786436
  4.6 0.8 %copy-start.4 = (f32[64,64]{1,0:T(8,128)S(1)}, f32[64,64]{1,0:T(8,128)}, u32[]{:S(2)}) copy-start(f32[64,64]{1,0:T(8,128)} %pre_in.1) | copy-start | bytes 49156
  5.3 0.8 %copy-start.5 = (f32[64,64]{1,0:T(8,128)S(1)}, f32[64,64]{1,0:T(8,128)}, u32[]{:S(2)}) copy-start(f32[64,64]{1,0:T(8,128)} %pre_out.1) | copy-start | bytes 49156
  6.1 0.7 %copy-start.6 = (s32[2]{0:T(128)S(1)}, s32[2]{0:T(128)}, u32[]{:S(2)}) copy-start(s32[2]{0:T(128)} %lengths.1) | copy-start | bytes 28

commit v2 on v1

--- a/solution.py
+++ b/solution.py
@@ -16,6 +16,20 @@
 
 def f32dot(a, b, dims):
     return lax.dot_general(a, b, dims, precision=HIGH, preferred_element_type=jnp.float32)
+
+
+def halves(a):
+    high = a.astype(jnp.bfloat16)
+    return high, (a - high.astype(jnp.float32)).astype(jnp.bfloat16)
+
+
+def split_dot(a, b, dims):
+    (ah, al), (bh, bl) = halves(a), halves(b)
+    return (
+        lax.dot_general(ah, bh, dims, preferred_element_type=jnp.float32)
+        + lax.dot_general(ah, bl, dims, preferred_element_type=jnp.float32)
+        + lax.dot_general(al, bh, dims, preferred_element_type=jnp.float32)
+    )
 
 
 def bf16dot(a, b):
@@ -54,6 +68,16 @@
         chips = nt // 2
         return ((t // 2 + chips - 1 - k // 2) % chips) * 2 + (t % 2 + 1 - k % 2) % 2
 
+    barrier = pltpu.get_barrier_semaphore()
+
+    def greet(name, place, size):
+        def one(i):
+            pl.semaphore_signal(barrier, inc=1, device_id={name: (place + i) % size}, device_id_type=MESH)
+        loop(1, size, one)
+
+    greet("dp", d, nd)
+    greet("tensor", t, nt)
+
     fixed = [
         pltpu.make_async_copy(src, dst, load_sem.at[2 * nt + i])
         for i, (src, dst) in enumerate(
@@ -73,20 +97,6 @@
             copy.start()
     fixed[4].start()
 
-    barrier = pltpu.get_barrier_semaphore()
-
-    def greet(i):
-        other = (d * nt + t + i) % total
-        pl.semaphore_signal(
-            barrier, inc=1, device_id={"dp": other // nt, "tensor": other % nt}, device_id_type=MESH
-        )
-
-    if total <= 16:
-        for i in range(1, total):
-            greet(i)
-    else:
-        loop(1, total, greet)
-
     for copy in fixed[:2]:
         copy.wait()
     r = lax.broadcasted_iota(jnp.int32, (width, width), 0)
@@ -102,15 +112,14 @@
             copy.wait()
         part[k, 0:width, 0:tok] = bf16dot(pin_v[...], acts_v[k])
         part[k, 0:tok, tok : tok + width] = bf16dot(grads_v[k], pout_v[...])
-        if k == 0:
-            pl.semaphore_wait(barrier, total - 1)
-        if k < nt - 1:
-            copy = pltpu.make_async_remote_copy(
-                src_ref=part.at[k], dst_ref=got.at[k], send_sem=send_a.at[k], recv_sem=recv_a.at[k],
-                device_id={"tensor": place(k)}, device_id_type=MESH,
-            )
-            copy.start()
-            sends.append(copy)
+    pl.semaphore_wait(barrier, nd + nt - 2)
+    for k in range(nt - 1):
+        copy = pltpu.make_async_remote_copy(
+            src_ref=part.at[k], dst_ref=got.at[k], send_sem=send_a.at[k], recv_sem=recv_a.at[k],
+            device_id={"tensor": place(k)}, device_id_type=MESH,
+        )
+        copy.start()
+        sends.append(copy)
     fixed[4].wait()
 
     left = part[nt - 1, 0:width, 0:tok]
@@ -123,9 +132,9 @@
     length = lengths[start // seq_len]
     slot = lax.broadcasted_iota(jnp.int32, (width, tok), 1) + start % seq_len
     left = jnp.where(slot < length, left, 0.0)
-    u = f32dot(pre_t, left, NN)
-    w = f32dot(right, pre_out_v[...], NT)
-    g = f32dot(u, w, NN)
+    u = split_dot(pre_t, left, NN)
+    w = split_dot(right, pre_out_v[...], NT)
+    g = split_dot(u, w, NN)
     gather[0] = jnp.concatenate([g[:half], g[half:]], axis=1)
 
     def gather_copy(j):
@@ -136,14 +145,15 @@
 
     loop(1, nd, lambda j: gather_copy(j).start())
 
-    ones = jnp.ones((8, 2 * width), jnp.float32)
+    ones = jnp.ones((8, 2 * width), jnp.bfloat16)
     mine = d * nt + t
 
     def score(j):
         acc = jnp.zeros((nq, 2 * width), jnp.float32)
         for p in range(half):
             acc = acc + query_v[:, 2 * width * p : 2 * width * (p + 1)] * gather[j, p : p + 1, :]
-        row = f32dot(ones, acc, NT)[0:1] * scale
+        high, low = halves(acc)
+        row = (bf16dot(ones, high) + bf16dot(ones, low))[0:1] * scale
         rows[j] = jnp.concatenate([row, row], axis=1)
 
     def row_copy(j, to):
@@ -221,7 +231,7 @@
                 dma((2 * nt + 5,)), dma((nt - 1,)), dma((nt - 1,)), dma((nd,)), dma((nd,)), dma, dma,
             ],
             compiler_params=pltpu.CompilerParams(
-                collective_id=0, has_side_effects=True, vmem_limit_bytes=48 * 1024 * 1024
+                collective_id=0, has_side_effects=True, vmem_limit_bytes=60 * 1024 * 1024
             ),
         )(lengths, acts, grads, pin.T, pout.T, query, pre_in, pre_out)
 

time: 27.4 us -> 21 us (0.77)
  local copies, waits for them, and re-layouts: 7.33 us -> 1.26 us
    unnamed x15 -> x1, local copies, waits for them, and re-layouts: 7.33 us -> 1.26 us
where the time goes in v2:
time: 21 us; the launch traced here: 20.9 us
  Pallas kernels  19.6 us (93%)
  local copies, waits for them, and re-layouts  1.26 us (6%)
    pallas_call x1, Pallas kernels, local(): pl.pallas_call(functools.partial(kernel, nd, nt, seq_len, scale), out_sha...  19.6 us
    unnamed x1, local copies, waits for them, and re-layouts  1.26 us

profile of v2, /device:TPU:0, one launch (start us, length us, event | category | flops | bytes accessed | tf_op | source)
XLA Modules:
  0.0 20.9 jit_solution(4589675258190191422)
XLA Ops:
  0.0 19.6 %shard_map.82 = f32[2,256]{1,0:T(2,128)} custom-call(s32[2]{0:T(128)} %lengths.1, bf16[256,7168]{1,0:T(8,128)(2,1)} %acts.1, bf16[256,2048]{1,0:T(8,128)(2,1)} %grads.1, bf16[64,7168]{1,0:T(8,128)(2,1)} %bitcast.2, bf16[64,2048]{1,0:T(8,128)(2,1)} %bitcast.3, f32[64,4096]{1,0:T(8,128)} %query.1, f32[64,64]{1,0:T(8,128)} %pre_in.1, f32[64,64]{1,0:T(8,128)} %pre_out.1), custom_call_target="tpu_custom_call" | custom-call | tf_op jit(solution)/shard_map/pallas_call | solution.py:213
  19.6 1.3 %copy.10 = f32[2,256]{1,0:T(2,128)} copy(f32[2,256]{1,0:T(2,128)} %shard_map.82) | data formatting | bytes 4096

commit v3 on v2

--- a/solution.py
+++ b/solution.py
@@ -112,14 +112,15 @@
             copy.wait()
         part[k, 0:width, 0:tok] = bf16dot(pin_v[...], acts_v[k])
         part[k, 0:tok, tok : tok + width] = bf16dot(grads_v[k], pout_v[...])
-    pl.semaphore_wait(barrier, nd + nt - 2)
-    for k in range(nt - 1):
-        copy = pltpu.make_async_remote_copy(
-            src_ref=part.at[k], dst_ref=got.at[k], send_sem=send_a.at[k], recv_sem=recv_a.at[k],
-            device_id={"tensor": place(k)}, device_id_type=MESH,
-        )
-        copy.start()
-        sends.append(copy)
+        if k == 0:
+            pl.semaphore_wait(barrier, nd + nt - 2)
+        if k < nt - 1:
+            copy = pltpu.make_async_remote_copy(
+                src_ref=part.at[k], dst_ref=got.at[k], send_sem=send_a.at[k], recv_sem=recv_a.at[k],
+                device_id={"tensor": place(k)}, device_id_type=MESH,
+            )
+            copy.start()
+            sends.append(copy)
     fixed[4].wait()
 
     left = part[nt - 1, 0:width, 0:tok]

time: 21 us -> 20.2 us (0.962)
  Pallas kernels: 19.6 us -> 18.7 us
    pallas_call x1, Pallas kernels: 19.6 us -> 18.7 us  [local(): pl.pallas_call(functools.partial(kernel, nd, nt, seq_len, scale), out_sha...]
where the time goes in v3:
time: 20.2 us; the launch traced here: 20 us
  Pallas kernels  18.7 us (93%)
  local copies, waits for them, and re-layouts  1.26 us (6%)
    pallas_call x1, Pallas kernels, local(): pl.pallas_call(functools.partial(kernel, nd, nt, seq_len, scale), out_sha...  18.7 us
    unnamed x1, local copies, waits for them, and re-layouts  1.26 us

profile of v3, /device:TPU:0, one launch (start us, length us, event | category | flops | bytes accessed | tf_op | source)
XLA Modules:
  0.0 20.0 jit_solution(2052999977240668401)
XLA Ops:
  0.0 18.7 %shard_map.82 = f32[2,256]{1,0:T(2,128)} custom-call(s32[2]{0:T(128)} %lengths.1, bf16[256,7168]{1,0:T(8,128)(2,1)} %acts.1, bf16[256,2048]{1,0:T(8,128)(2,1)} %grads.1, bf16[64,7168]{1,0:T(8,128)(2,1)} %bitcast.2, bf16[64,2048]{1,0:T(8,128)(2,1)} %bitcast.3, f32[64,4096]{1,0:T(8,128)} %query.1, f32[64,64]{1,0:T(8,128)} %pre_in.1, f32[64,64]{1,0:T(8,128)} %pre_out.1), custom_call_target="tpu_custom_call" | custom-call | tf_op jit(solution)/shard_map/pallas_call | solution.py:214
  18.7 1.3 %copy.10 = f32[2,256]{1,0:T(2,128)} copy(f32[2,256]{1,0:T(2,128)} %shard_map.82) | data formatting | bytes 4096

commit v4 on v3

--- a/solution.py
+++ b/solution.py
@@ -112,15 +112,17 @@
             copy.wait()
         part[k, 0:width, 0:tok] = bf16dot(pin_v[...], acts_v[k])
         part[k, 0:tok, tok : tok + width] = bf16dot(grads_v[k], pout_v[...])
-        if k == 0:
+        if k == 1:
             pl.semaphore_wait(barrier, nd + nt - 2)
         if k < nt - 1:
             copy = pltpu.make_async_remote_copy(
                 src_ref=part.at[k], dst_ref=got.at[k], send_sem=send_a.at[k], recv_sem=recv_a.at[k],
                 device_id={"tensor": place(k)}, device_id_type=MESH,
             )
-            copy.start()
             sends.append(copy)
+        if k >= 1:
+            for copy in sends[0 if k == 1 else k : k + 1]:
+                copy.start()
     fixed[4].wait()
 
     left = part[nt - 1, 0:width, 0:tok]

time: 20.2 us -> 19.9 us (0.985)
    pallas_call x1, Pallas kernels: 18.7 us -> 18.5 us  [local(): pl.pallas_call(functools.partial(kernel, nd, nt, seq_len, scale), out_sha...]
where the time goes in v4:
time: 19.9 us; the launch traced here: 19.7 us
  Pallas kernels  18.5 us (93%)
  local copies, waits for them, and re-layouts  1.26 us (6%)
    pallas_call x1, Pallas kernels, local(): pl.pallas_call(functools.partial(kernel, nd, nt, seq_len, scale), out_sha...  18.5 us
    unnamed x1, local copies, waits for them, and re-layouts  1.26 us

profile of v4, /device:TPU:0, one launch (start us, length us, event | category | flops | bytes accessed | tf_op | source)
XLA Modules:
  0.0 19.7 jit_solution(10420439480447947659)
XLA Ops:
  0.0 18.5 %shard_map.82 = f32[2,256]{1,0:T(2,128)} custom-call(s32[2]{0:T(128)} %lengths.1, bf16[256,7168]{1,0:T(8,128)(2,1)} %acts.1, bf16[256,2048]{1,0:T(8,128)(2,1)} %grads.1, bf16[64,7168]{1,0:T(8,128)(2,1)} %bitcast.2, bf16[64,2048]{1,0:T(8,128)(2,1)} %bitcast.3, f32[64,4096]{1,0:T(8,128)} %query.1, f32[64,64]{1,0:T(8,128)} %pre_in.1, f32[64,64]{1,0:T(8,128)} %pre_out.1), custom_call_target="tpu_custom_call" | custom-call | tf_op jit(solution)/shard_map/pallas_call | solution.py:216
  18.5 1.3 %copy.10 = f32[2,256]{1,0:T(2,128)} copy(f32[2,256]{1,0:T(2,128)} %shard_map.82) | data formatting | bytes 4096
